TPU v7x, 256 devices: a whole 4x4x8 slice. The times are simulated.
256 devices in a mesh: dp: 2 (over core), seq: 16 (over z_lo, x), chan: 8 (over y, z_hi).
Axes of the slice: x: 4, y: 4, z: 8 (z_hi: 2, z_lo: 4; z = z_hi * 4 + z_lo), core: 2. Of those that a mesh axis runs over, the one named last changes fastest.
Arguments:
- tokens: bfloat16 [1, 8192, 4096], P(None, ('dp', 'seq'), 'chan'), may hold values from -6 to 6
- w_value: bfloat16 [4096, 4096], P(None, 'chan'), may hold values from -0.09375 to 0.09375
- gate_k: bfloat16 [1, 8192, 4096], P(None, ('dp', 'seq'), 'chan'), may hold values from -5 to 5
- gate_q: bfloat16 [1, 8192, 4096], P(None, ('dp', 'seq'), 'chan'), may hold values from -5 to 5
- filter_weight: float32 [64, 4096], P(None, 'chan'), may hold values from -6 to 6
- decay: float32 [4096], P('chan'), may hold values from 0.5 to 8
- skip_bias: float32 [4096], P('chan'), may hold values from 0.5 to 1.5
- cotangent: bfloat16 [1, 8192, 4096], P(None, ('dp', 'seq'), 'chan'), may hold values from -16 to 16
Outputs:
- mixed: bfloat16 [1, 8192, 4096], P(None, ('dp', 'seq'), 'chan')
- grad_tokens: bfloat16 [1, 8192, 4096], P(None, ('dp', 'seq'), 'chan')
- grad_gate_k: bfloat16 [1, 8192, 4096], P(None, ('dp', 'seq'), 'chan')
- grad_gate_q: bfloat16 [1, 8192, 4096], P(None, ('dp', 'seq'), 'chan')
- grad_filter: float32 [64, 4096], P(None, 'chan')
- grad_bias: float32 [4096], P('chan')
All inputs are finite; a program needn't handle non-finite values.
Results may differ from a plain program's by a relative error of at most 0.012.
Values may be sent and summed in bfloat16 or wider, within the bound.
A program may use at most 128 MiB of HBM per device.

v0:
```python
import math
import jax
import jax.numpy as jnp
import numpy as np
from jax import lax
from jax.sharding import PartitionSpec as P

BF = jnp.bfloat16
F32 = jnp.float32


def tables(block, order):
    pos = np.arange(block, dtype=np.float64)
    harm = 2.0 * np.pi / block * np.arange(1, order + 1, dtype=np.float64)
    half = np.pi / block * (2.0 * np.arange(block // 2, dtype=np.float64) + 1.0)
    even = harm[:, None] * pos[None, :]
    odd = half[:, None] * pos[None, :]
    dft = np.concatenate([np.cos(even), np.sin(even), np.cos(odd), np.sin(odd)])
    cross = np.sin(odd) @ np.cos(even).T
    return (dft.astype(np.float32), cross.astype(np.float32))


def dot(a, b):
    return jnp.dot(a.astype(BF), b.astype(BF), preferred_element_type=F32)


def body(tokens, w_value, gate_k, gate_q, filter_weight, decay, skip_bias, cotangent):
    tok = tokens[0]
    block, width = tok.shape
    groups = lax.axis_size(("dp", "seq"))
    index = lax.axis_index(("dp", "seq"))
    length = block * groups
    order = filter_weight.shape[0]
    scale = 1.0 / math.sqrt(order * length)
    dft_np, cross_np = tables(block, order)
    dft = jnp.asarray(dft_np)
    cross = jnp.asarray(cross_np)
    n_even = 2 * order
    half = block // 2
    values = (
        jnp.dot(
            lax.all_gather(tok, "chan", axis=1, tiled=True), w_value, preferred_element_type=F32
        )
        .astype(BF)
        .astype(F32)
    )
    key = gate_k[0].astype(F32)
    query = gate_q[0].astype(F32)
    inc = cotangent[0].astype(F32)
    mixed_in = key * values
    grad_state = query * inc
    pos = jnp.arange(block, dtype=F32)[:, None] / length
    fade = jnp.exp(-pos * decay[None, :])
    grow = jnp.exp(pos * decay[None, :])
    x_spec = dot(dft, mixed_in * grow)
    g_spec = dot(dft, grad_state * fade)
    weights = filter_weight * scale
    kern_c = jnp.sum(weights, axis=0, keepdims=True)
    kern_s = jnp.dot(cross, weights, precision=lax.Precision.HIGHEST)
    states = jnp.concatenate([x_spec[:n_even], g_spec[:n_even]])
    sub = width // groups
    mine = lax.all_to_all(
        states.reshape(2 * n_even, groups, sub),
        ("dp", "seq"),
        split_axis=1,
        concat_axis=1,
        tiled=True,
    )
    dec = lax.dynamic_slice_in_dim(decay, index * sub, sub, 0)
    ids = jnp.arange(groups)
    gap = (ids[:, None] - ids[None, :]).astype(F32)
    low = jnp.where(
        gap[:, :, None] > 0,
        jnp.exp(-jnp.maximum(gap, 0.0)[:, :, None] * dec * (block / length)),
        0.0,
    )
    carried_x = jnp.einsum("ijc,rjc->ric", low, mine[:n_even], precision=lax.Precision.HIGHEST)
    carried_g = jnp.einsum("jic,rjc->ric", low, mine[n_even:], precision=lax.Precision.HIGHEST)
    back = lax.all_to_all(
        jnp.concatenate([carried_x, carried_g]),
        ("dp", "seq"),
        split_axis=1,
        concat_axis=1,
        tiled=True,
    ).reshape(2 * n_even, width)
    z_x, z_g = (back[:n_even], back[n_even:])
    two = jnp.concatenate([weights, weights])
    xe, ge = (x_spec[:n_even], g_spec[:n_even])
    xc, xs = (x_spec[n_even : n_even + half], x_spec[n_even + half :])
    gc, gs = (g_spec[n_even : n_even + half], g_spec[n_even + half :])
    inv = 1.0 / block
    y_spec = jnp.concatenate(
        [
            two * (z_x + 0.5 * xe),
            inv * (kern_c * xc - kern_s * xs),
            inv * (kern_c * xs + kern_s * xc),
        ]
    )
    p_spec = jnp.concatenate(
        [
            two * (z_g + 0.5 * ge),
            inv * (kern_c * gc + kern_s * gs),
            inv * (kern_c * gs - kern_s * gc),
        ]
    )
    gated_state = fade * dot(dft.T, y_spec) + skip_bias * mixed_in
    grad_in = grow * dot(dft.T, p_spec) + skip_bias * grad_state
    n_c = gc * xc + gs * xs
    n_s = gs * xc - gc * xs
    prod = ge * (z_x + 0.5 * xe)
    part = scale * (
        prod[:order]
        + prod[order:]
        + inv
        * (
            jnp.sum(n_c, axis=0, keepdims=True)
            + jnp.dot(cross.T, n_s, precision=lax.Precision.HIGHEST)
        )
    )
    part_bias = jnp.sum(mixed_in * grad_state, axis=0, keepdims=True)
    sums = lax.psum(jnp.concatenate([part, part_bias]), ("dp", "seq"))
    mixed = (query * gated_state).astype(BF)
    grad_values = (key * grad_in).astype(BF)
    terms = lax.dot_general(
        grad_values, w_value, (((1,), (1,)), ((), ())), preferred_element_type=F32
    )
    grad_tok = lax.psum_scatter(terms, "chan", scatter_dimension=1, tiled=True).astype(BF)
    grad_key = (values * grad_in).astype(BF)
    grad_query = (gated_state * inc).astype(BF)
    return (
        mixed[None],
        grad_tok[None],
        grad_key[None],
        grad_query[None],
        sums[:order],
        sums[order],
    )


def solution(mesh):
    rows = P(None, ("dp", "seq"), "chan")
    cols = P(None, "chan")
    return jax.shard_map(
        body,
        mesh=mesh,
        in_specs=(rows, cols, rows, rows, cols, P("chan"), P("chan"), rows),
        out_specs=(rows, rows, rows, rows, cols, P("chan")),
        check_vma=False,
    )
```

profile of v0, /device:TPU:2, one launch (start us, length us, event | category | flops | bytes accessed | tf_op | source)
XLA Modules:
  0.0 545.9 jit_solution(2549810589941749096)
XLA Ops:
  7.2 0.7 all-gather.3.cloned.1.call-update
  7.9 1.5 fusion.20
  9.5 80.6 %all-gather.3.cloned.1.call-done = bf16[1,256,4096]{2,1,0:T(8,128)(2,1)} async-done(((bf16[1,256,512]{2,1,0:T(8,128)(2,1)}), bf16[1,256,4096]{2,1,0:T(8,128)(2,1)}) %all-gather.3.cloned.1.call-update) | async-done | bytes 2097168 | tf_op jit(solution)/shard_map/all_gather | solution.py:42
  90.1 4.1 fusion.9
  94.2 0.4 fusion.19
  94.7 1.0 copy.27
  95.7 5.7 %all-to-all-start = ((f32[256,32,16]{0,2,1:T(8,128)}), f32[256,32,16]{0,2,1:T(8,128)S(1)}, u32[]{:S(2)}, u32[]{:S(2)}) async-start(f32[256,32,16]{0,2,1:T(8,128)} %bitcast.5), calls=%async_computation | async-start | bytes 1048576 | tf_op jit(solution)/shard_map/all_to_all | solution.py:62
  101.5 14.9 %all-to-all-done = f32[256,32,16]{0,2,1:T(8,128)S(1)} async-done(((f32[256,32,16]{0,2,1:T(8,128)}), f32[256,32,16]{0,2,1:T(8,128)S(1)}, u32[]{:S(2)}, u32[]{:S(2)}) %all-to-all-start) | async-done | bytes 524320 | tf_op jit(solution)/shard_map/all_to_all | solution.py:62
  116.4 0.7 convolution_bitcast_fusion.1
  117.1 0.5 convolution_bitcast_fusion
  117.6 1.1 copy.31
  118.7 5.9 %all-to-all-start.1 = ((f32[256,32,16]{0,2,1:T(8,128)}), f32[256,32,16]{0,2,1:T(8,128)S(1)}, u32[]{:S(2)}, u32[]{:S(2)}) async-start(f32[256,32,16]{0,2,1:T(8,128)} %copy.31), calls=%async_computation.1 | async-start | bytes 1048576 | tf_op jit(solution)/shard_map/all_to_all | solution.py:79
  124.8 0.4 fusion.83
  125.2 14.6 %all-to-all-done.1 = f32[256,32,16]{0,2,1:T(8,128)S(1)} async-done(((f32[256,32,16]{0,2,1:T(8,128)}), f32[256,32,16]{0,2,1:T(8,128)S(1)}, u32[]{:S(2)}, u32[]{:S(2)}) %all-to-all-start.1) | async-done | bytes 524320 | tf_op jit(solution)/shard_map/all_to_all | solution.py:79
  139.7 0.7 fusion.87
  140.5 1.1 copy.33
  141.6 0.1 copy.32
  141.8 0.2 add_reduce_fusion
  142.0 1.1 fusion.48
  143.1 1.1 fusion.46
  144.2 0.2 convolution_add_fusion.1
  144.4 0.2 convolution_add_fusion.3
  144.7 0.3 fusion.15
  145.1 0.3 fusion.5
  145.4 1.3 fusion.22
  146.7 0.7 pad_maximum_fusion.3
  147.5 5.4 fusion.23
  152.9 251.9 %all-reduce.2.cloned.1.call-done = f32[65,512]{1,0:T(8,128)} async-done(((f32[65,512]{1,0:T(8,128)}), f32[65,512]{1,0:T(8,128)}) %all-reduce.2.cloned.1.call-update) | async-done | bytes 133136 | tf_op jit(solution)/shard_map/psum | solution.py:121
  404.8 1.3 slice.85
  406.1 1.6 slice.84
  407.7 130.0 %reduce-scatter.2.cloned.1.call-done = f32[256,512]{1,0:T(8,128)} async-done(((f32[256,4096]{1,0:T(8,128)}), f32[256,512]{1,0:T(8,128)}) %reduce-scatter.2.cloned.1.call-update) | async-done | bytes 524304 | tf_op jit(solution)/shard_map/reduce_scatter | solution.py:127
  537.6 1.8 convert_bitcast_fusion
  (38 shorter events, 0.5 us)
Async XLA Ops:
  7.2 82.9 %all-gather.3.cloned.1.call-start = ((), (), s32[]{:S(2)}) async-start(), calls=%async_computation.5 | async-start | bytes 2359296 | tf_op jit(solution)/shard_map/all_gather | solution.py:42
  9.4 84.7 %copy-start.2 = (bf16[1,256,512]{2,1,0:T(8,128)(2,1)S(1)}, bf16[1,256,512]{2,1,0:T(8,128)(2,1)}, u32[]{:S(2)}) copy-start(bf16[1,256,512]{2,1,0:T(8,128)(2,1)} %param.12) | copy-start | bytes 786436
  9.4 84.7 %copy-start.3 = (bf16[384,256]{1,0:T(8,128)(2,1)S(1)}, bf16[384,256]{1,0:T(8,128)(2,1)}, u32[]{:S(2)}) copy-start(bf16[384,256]{1,0:T(8,128)(2,1)} %constant.40) | copy-start | bytes 589828
  9.5 84.7 %copy-start.9 = (f32[512]{0:T(512)S(1)}, f32[512]{0:T(512)}, u32[]{:S(2)}) copy-start(f32[512]{0:T(512)} %param.15) | copy-start | bytes 6148
  94.6 30.1 %copy-start.4 = (f32[64,512]{1,0:T(8,128)S(1)}, f32[64,512]{1,0:T(8,128)}, u32[]{:S(2)}) copy-start(f32[64,512]{1,0:T(8,128)} %param.14) | copy-start | bytes 393220
  94.6 30.1 %copy-start.7 = (f32[128,64]{1,0:T(8,128)S(1)}, f32[128,64]{1,0:T(8,128)}, u32[]{:S(2)}) copy-start(f32[128,64]{1,0:T(8,128)} %constant.39.clone) | copy-start | bytes 98308
  95.7 20.7 %all-to-all-start = ((f32[256,32,16]{0,2,1:T(8,128)}), f32[256,32,16]{0,2,1:T(8,128)S(1)}, u32[]{:S(2)}, u32[]{:S(2)}) async-start(f32[256,32,16]{0,2,1:T(8,128)} %bitcast.5), calls=%async_computation | async-start | bytes 1048576 | tf_op jit(solution)/shard_map/all_to_all | solution.py:62
  118.7 21.0 %all-to-all-start.1 = ((f32[256,32,16]{0,2,1:T(8,128)}), f32[256,32,16]{0,2,1:T(8,128)S(1)}, u32[]{:S(2)}, u32[]{:S(2)}) async-start(f32[256,32,16]{0,2,1:T(8,128)} %copy.31), calls=%async_computation.1 | async-start | bytes 1048576 | tf_op jit(solution)/shard_map/all_to_all | solution.py:79
  124.7 280.1 %all-reduce.2.cloned.1.call-start = ((), (), s32[]{:S(2)}) async-start(), calls=%async_computation.4 | async-start | bytes 294912 | tf_op jit(solution)/shard_map/psum | solution.py:121
  141.7 2.5 copy-start.6
  141.7 3.0 copy-start.8
  141.7 3.3 copy-start
  141.7 3.3 copy-start.1
  141.7 3.3 copy-start.5
  141.8 3.3 copy-start.10
  147.4 390.2 %reduce-scatter.2.cloned.1.call-start = ((), (), s32[]{:S(2)}) async-start(), calls=%async_computation.3 | async-start | bytes 4718592 | tf_op jit(solution)/shard_map/reduce_scatter | solution.py:127
Sparse Core Ops, SparseCore 0:
  10.5 79.5 all-gather.2
  147.5 257.2 all-reduce.1
  409.6 128.0 reduce-scatter.1
where the time goes:
time: 546 us
  waiting for transfers between devices  493 us (90%)
  matrix products  17.5 us (3%)
  between operations  14.1 us (3%)
  starting transfers between devices  11.7 us (2%)
  local copies, waits for them, and re-layouts  7.12 us (1%)
    psum x1, waiting for transfers between devices, body(): sums = lax.psum(jnp.concatenate([part, part_bias]), ('dp', 'seq'))  252 us
    reduce_scatter x1, waiting for transfers between devices, body(): lax.psum_scatter(terms, 'chan', scatter_dimension=1, tiled=True).astype(BF)  130 us
    all_gather x1, waiting for transfers between devices, body(): lax.all_gather(tok, 'chan', axis=1, tiled=True)  80.6 us
    all_to_all x1, waiting for transfers between devices, body(): lax.all_to_all(states.reshape(2 * n_even, groups, sub), ('dp', 'seq'), sp...  14.9 us
    all_to_all x1, waiting for transfers between devices, body(): lax.all_to_all(jnp.concatenate([carried_x, carried_g]), ('dp', 'seq'), sp...  14.6 us
  transfers between devices with their start and end apart: 5, of which 5 were waited for; matrix products, arithmetic and copies ran while one was open for 2% of the time, Pallas kernels for 0%

commit v1 on v0

--- a/solution.py
+++ b/solution.py
@@ -118,7 +118,7 @@
         )
     )
     part_bias = jnp.sum(mixed_in * grad_state, axis=0, keepdims=True)
-    sums = lax.psum(jnp.concatenate([part, part_bias]), ("dp", "seq"))
+    sums = lax.psum(lax.psum(jnp.concatenate([part, part_bias]), "seq"), "dp")
     mixed = (query * gated_state).astype(BF)
     grad_values = (key * grad_in).astype(BF)
     terms = lax.dot_general(

time: 546 us -> 468 us (0.86)
  waiting for transfers between devices: 493 us -> 411 us
    psum x1 -> x2, waiting for transfers between devices: 252 us -> 170 us  [body(): sums = lax.psum(lax.psum(jnp.concatenate([part, part_bias]), 'seq'), 'dp')]
  transfers between devices with their start and end apart: 5 -> 6, of which waited for: 5 -> 6; matrix products, arithmetic and copies ran while one was open for 2% -> 2% of each run, Pallas kernels for 0% -> 0%
where the time goes in v1:
time: 468 us; the launch traced here: 467 us
  waiting for transfers between devices  411 us (88%)
  matrix products  19.2 us (4%)
  between operations  14.1 us (3%)
  starting transfers between devices  11.8 us (3%)
  local copies, waits for them, and re-layouts  8.16 us (2%)
    psum x2, waiting for transfers between devices, body(): sums = lax.psum(lax.psum(jnp.concatenate([part, part_bias]), 'seq'), 'dp')  170 us
    reduce_scatter x1, waiting for transfers between devices, body(): lax.psum_scatter(terms, 'chan', scatter_dimension=1, tiled=True).astype(BF)  130 us
    all_gather x1, waiting for transfers between devices, body(): lax.all_gather(tok, 'chan', axis=1, tiled=True)  80.6 us
    all_to_all x1, waiting for transfers between devices, body(): lax.all_to_all(states.reshape(2 * n_even, groups, sub), ('dp', 'seq'), sp...  14.9 us
    all_to_all x1, waiting for transfers between devices, body(): lax.all_to_all(jnp.concatenate([carried_x, carried_g]), ('dp', 'seq'), sp...  14.6 us
  transfers between devices with their start and end apart: 6, of which 6 were waited for; matrix products, arithmetic and copies ran while one was open for 2% of the time, Pallas kernels for 0%

profile of v1, /device:TPU:2, one launch (start us, length us, event | category | flops | bytes accessed | tf_op | source)
XLA Modules:
  0.0 467.5 jit_solution(2915181425238740061)
XLA Ops:
  7.2 0.7 all-gather.3.cloned.1.call-update
  7.9 1.5 fusion.20
  9.5 80.6 %all-gather.3.cloned.1.call-done = bf16[1,256,4096]{2,1,0:T(8,128)(2,1)} async-done(((bf16[1,256,512]{2,1,0:T(8,128)(2,1)}), bf16[1,256,4096]{2,1,0:T(8,128)(2,1)}) %all-gather.3.cloned.1.call-update) | async-done | bytes 2097168 | tf_op jit(solution)/shard_map/all_gather | solution.py:42
  90.1 4.1 fusion.9
  94.2 0.4 fusion.19
  94.7 1.0 copy.27
  95.7 5.7 %all-to-all-start = ((f32[256,32,16]{0,2,1:T(8,128)}), f32[256,32,16]{0,2,1:T(8,128)S(1)}, u32[]{:S(2)}, u32[]{:S(2)}) async-start(f32[256,32,16]{0,2,1:T(8,128)} %bitcast.5), calls=%async_computation | async-start | bytes 1048576 | tf_op jit(solution)/shard_map/all_to_all | solution.py:62
  101.5 14.9 %all-to-all-done = f32[256,32,16]{0,2,1:T(8,128)S(1)} async-done(((f32[256,32,16]{0,2,1:T(8,128)}), f32[256,32,16]{0,2,1:T(8,128)S(1)}, u32[]{:S(2)}, u32[]{:S(2)}) %all-to-all-start) | async-done | bytes 524320 | tf_op jit(solution)/shard_map/all_to_all | solution.py:62
  116.4 0.7 convolution_bitcast_fusion.1
  117.1 0.5 convolution_bitcast_fusion
  117.6 1.1 copy.31
  118.7 5.9 %all-to-all-start.1 = ((f32[256,32,16]{0,2,1:T(8,128)}), f32[256,32,16]{0,2,1:T(8,128)S(1)}, u32[]{:S(2)}, u32[]{:S(2)}) async-start(f32[256,32,16]{0,2,1:T(8,128)} %copy.31), calls=%async_computation.1 | async-start | bytes 1048576 | tf_op jit(solution)/shard_map/all_to_all | solution.py:79
  124.8 0.4 fusion.83
  125.1 14.6 %all-to-all-done.1 = f32[256,32,16]{0,2,1:T(8,128)S(1)} async-done(((f32[256,32,16]{0,2,1:T(8,128)}), f32[256,32,16]{0,2,1:T(8,128)S(1)}, u32[]{:S(2)}, u32[]{:S(2)}) %all-to-all-start.1) | async-done | bytes 524320 | tf_op jit(solution)/shard_map/all_to_all | solution.py:79
  139.7 0.8 fusion.87
  140.6 1.1 copy.33
  141.6 1.1 copy.32
  143.0 1.1 fusion.48
  144.1 1.1 fusion.46
  145.2 1.1 convolution_add_fusion.1
  146.3 1.1 convolution_add_fusion.3
  147.4 0.3 fusion.15
  147.8 0.3 fusion.5
  148.1 1.3 fusion.22
  149.4 0.7 pad_maximum_fusion.3
  150.2 145.0 %all-reduce.3.cloned.1.call-done = f32[65,512]{1,0:T(8,128)} async-done(((f32[65,512]{1,0:T(8,128)}), f32[65,512]{1,0:T(8,128)}) %all-reduce.3.cloned.1.call-update) | async-done | bytes 133136 | tf_op jit(solution)/shard_map/psum | solution.py:121
  295.2 5.4 %fusion.23 = f32[256,4096]{1,0:T(8,128)} fusion(bf16[4096,512]{1,0:T(8,128)(2,1)} %param.11, f32[256,512]{1,0:T(8,128)S(1)} %fusion.5, bf16[1,256,512]{2,1,0:T(8,128)(2,1)S(1)} %copy-done.2), kind=kOutput, calls=%fused_computation.39 | convolution fusion | flops 1074135040 | bytes 9175040 | tf_op jit(solution)/shard_map/dot_general | solution.py:124
  300.7 25.4 %all-reduce.5.cloned.1.call-done = f32[65,512]{1,0:T(8,128)} async-done(((f32[65,512]{1,0:T(8,128)}), f32[65,512]{1,0:T(8,128)}) %all-reduce.5.cloned.1.call-update) | async-done | bytes 133136 | tf_op jit(solution)/shard_map/psum | solution.py:121
  326.1 1.3 slice.85
  327.4 1.6 slice.84
  329.0 130.2 %reduce-scatter.2.cloned.1.call-done = f32[256,512]{1,0:T(8,128)} async-done(((f32[256,4096]{1,0:T(8,128)}), f32[256,512]{1,0:T(8,128)}) %reduce-scatter.2.cloned.1.call-update) | async-done | bytes 524304 | tf_op jit(solution)/shard_map/reduce_scatter | solution.py:127
  459.2 1.8 convert_bitcast_fusion
  (39 shorter events, 0.8 us)
Async XLA Ops:
  7.2 82.9 %all-gather.3.cloned.1.call-start = ((), (), s32[]{:S(2)}) async-start(), calls=%async_computation.6 | async-start | bytes 2359296 | tf_op jit(solution)/shard_map/all_gather | solution.py:42
  9.4 84.7 %copy-start.2 = (bf16[1,256,512]{2,1,0:T(8,128)(2,1)S(1)}, bf16[1,256,512]{2,1,0:T(8,128)(2,1)}, u32[]{:S(2)}) copy-start(bf16[1,256,512]{2,1,0:T(8,128)(2,1)} %param.12) | copy-start | bytes 786436
  9.4 84.7 %copy-start.3 = (bf16[384,256]{1,0:T(8,128)(2,1)S(1)}, bf16[384,256]{1,0:T(8,128)(2,1)}, u32[]{:S(2)}) copy-start(bf16[384,256]{1,0:T(8,128)(2,1)} %constant.40) | copy-start | bytes 589828
  9.5 84.7 %copy-start.8 = (f32[512]{0:T(512)S(1)}, f32[512]{0:T(512)}, u32[]{:S(2)}) copy-start(f32[512]{0:T(512)} %param.15) | copy-start | bytes 6148
  94.6 30.1 %copy-start.4 = (f32[64,512]{1,0:T(8,128)S(1)}, f32[64,512]{1,0:T(8,128)}, u32[]{:S(2)}) copy-start(f32[64,512]{1,0:T(8,128)} %param.14) | copy-start | bytes 393220
  94.6 30.2 %copy-start.6 = (f32[128,64]{1,0:T(8,128)S(1)}, f32[128,64]{1,0:T(8,128)}, u32[]{:S(2)}) copy-start(f32[128,64]{1,0:T(8,128)} %constant.39.clone) | copy-start | bytes 98308
  95.7 20.7 %all-to-all-start = ((f32[256,32,16]{0,2,1:T(8,128)}), f32[256,32,16]{0,2,1:T(8,128)S(1)}, u32[]{:S(2)}, u32[]{:S(2)}) async-start(f32[256,32,16]{0,2,1:T(8,128)} %bitcast.5), calls=%async_computation | async-start | bytes 1048576 | tf_op jit(solution)/shard_map/all_to_all | solution.py:62
  118.7 21.0 %all-to-all-start.1 = ((f32[256,32,16]{0,2,1:T(8,128)}), f32[256,32,16]{0,2,1:T(8,128)S(1)}, u32[]{:S(2)}, u32[]{:S(2)}) async-start(f32[256,32,16]{0,2,1:T(8,128)} %copy.31), calls=%async_computation.1 | async-start | bytes 1048576 | tf_op jit(solution)/shard_map/all_to_all | solution.py:79
  124.7 170.5 %all-reduce.3.cloned.1.call-start = ((), (), s32[]{:S(2)}) async-start(), calls=%async_computation.4 | async-start | bytes 294912 | tf_op jit(solution)/shard_map/psum | solution.py:121
  142.7 4.6 copy-start.7
  142.7 5.0 %copy-start = (bf16[1,256,512]{2,1,0:T(8,128)(2,1)S(1)}, bf16[1,256,512]{2,1,0:T(8,128)(2,1)}, u32[]{:S(2)}) copy-start(bf16[1,256,512]{2,1,0:T(8,128)(2,1)} %param.17) | copy-start | bytes 786436
  142.8 5.0 %copy-start.1 = (bf16[1,256,512]{2,1,0:T(8,128)(2,1)S(1)}, bf16[1,256,512]{2,1,0:T(8,128)(2,1)}, u32[]{:S(2)}) copy-start(bf16[1,256,512]{2,1,0:T(8,128)(2,1)} %param.13) | copy-start | bytes 786436
  142.8 5.0 %copy-start.5 = (bf16[128,256]{1,0:T(8,128)(2,1)S(1)}, bf16[128,256]{1,0:T(8,128)(2,1)}, u32[]{:S(2)}) copy-start(bf16[128,256]{1,0:T(8,128)(2,1)} %constant.43) | copy-start | bytes 196612
  142.8 5.0 %copy-start.9 = (f32[512]{0:T(512)S(1)}, f32[512]{0:T(512)}, u32[]{:S(2)}) copy-start(f32[512]{0:T(512)} %param.16) | copy-start | bytes 6148
  150.1 176.0 %all-reduce.5.cloned.1.call-start = ((), (), s32[]{:S(2)}) async-start(), calls=%async_computation.5 | async-start | bytes 294912 | tf_op jit(solution)/shard_map/psum | solution.py:121
  295.2 164.0 %reduce-scatter.2.cloned.1.call-start = ((), (), s32[]{:S(2)}) async-start(), calls=%async_computation.3 | async-start | bytes 4718592 | tf_op jit(solution)/shard_map/reduce_scatter | solution.py:127
Sparse Core Ops, SparseCore 0:
  10.5 79.5 all-gather.2
  150.2 144.8 all-reduce.2
  297.9 28.1 all-reduce.4
  330.7 128.4 reduce-scatter.1
